TPU v7x, 32 devices: a whole 2x2x4 slice. The times are simulated.
32 devices in a mesh: vec: 8 (over y, x, core), field: 4 (over z).
Axes of the slice: x: 2, y: 2, z: 4, core: 2. Of those that a mesh axis runs over, the one named last changes fastest.
Arguments:
- vectors: float32 [512, 6144], P('vec', 'field'), may hold values from -6 to 6
Outputs:
- first_tensor: float32 [512, 4096], P(('vec', 'field'))
- second_tensor: float32 [512, 4096], P(('vec', 'field'))
All inputs are finite; a program needn't handle non-finite values.
Results may differ from a plain program's by a relative error of at most 0.000098.
Values sent between devices are 32-bit elements; how exact they have to be, the bound alone decides.
A program may use at most 64 MiB of HBM per device.

v0:
```python
import math

import jax
import jax.numpy as jnp
from jax import lax
from jax.sharding import PartitionSpec as P


def passed_along(x, axis, by):
    peers = lax.axis_size(axis)
    return lax.ppermute(x, axis, [(i, (i + by) % peers) for i in range(peers)])


def triple_rows(a_rows, partner, third):
    count = a_rows.shape[0]
    group_size = math.gcd(count, 8)
    groups = a_rows.reshape(count // group_size, group_size, a_rows.shape[1])

    def single_group(group):
        product = (group[:, None, :] * partner[None, :, :]).reshape(
            group_size * partner.shape[0], group.shape[1]
        )
        result = lax.dot_general(
            product,
            third,
            (((1,), (1,)), ((), ())),
            precision=lax.Precision.HIGHEST,
            preferred_element_type=jnp.float32,
        )
        return result.reshape(group_size, partner.shape[0] * third.shape[0])

    return lax.map(single_group, groups).reshape(count, partner.shape[0] * third.shape[0])


def per_device(vectors):
    parts = lax.axis_size("field")
    block_rows = vectors.shape[0]
    owned = block_rows // parts
    scale = 1.0 / math.sqrt(vectors.shape[1] * parts)
    following = passed_along(vectors, "vec", -1)
    further = passed_along(vectors, "vec", -2)
    first_tensor = (
        lax.psum_scatter(
            triple_rows(vectors, following, further), "field", scatter_dimension=0, tiled=True
        )
        * scale
    )
    earlier = passed_along(first_tensor, "vec", 1)
    earlier = earlier.reshape(owned, parts, owned * block_rows)
    turned = lax.all_to_all(earlier, "field", split_axis=1, concat_axis=0, tiled=True)
    turned = turned.reshape(block_rows, owned, block_rows)
    second_tensor = jnp.transpose(turned, (1, 0, 2)).reshape(owned, block_rows * block_rows)
    return (first_tensor, second_tensor)


def solution(mesh):
    placed = (P("vec", "field"),)
    return jax.shard_map(
        per_device,
        mesh=mesh,
        in_specs=placed,
        out_specs=(P(("vec", "field"), None), P(("vec", "field"), None)),
        check_vma=False,
    )
```

profile of v0, /device:TPU:0, one launch (start us, length us, event | category | flops | bytes accessed | tf_op | source)
XLA Modules:
  0.0 116.4 jit_solution(11658642691268801528)
XLA Ops:
  7.2 0.0 reduce-scatter.2.cloned.1.call-start
  7.2 3.4 %collective-permute-start = (f32[64,1536]{1,0:T(8,128)}, f32[64,1536]{1,0:T(8,128)S(1)}, u32[]{:S(2)}, u32[]{:S(2)}) collective-permute-start(f32[64,1536]{1,0:T(8,128)} %param.3), channel_id=1, source_target_pairs={{0,28},{4,0},{8,4},{12,8},{16,12},{20,16},{24,20},{28,24},{1,29},{... | collective-permute-start | bytes 1179656 | tf_op jit(solution)/shard_map/ppermute | solution.py:11
  10.6 0.6 collective-permute-start.1
  11.2 9.1 %collective-permute-done = f32[64,1536]{1,0:T(8,128)S(1)} collective-permute-done((f32[64,1536]{1,0:T(8,128)}, f32[64,1536]{1,0:T(8,128)S(1)}, u32[]{:S(2)}, u32[]{:S(2)}) %collective-permute-start) | collective-permute-done | bytes 393248 | tf_op jit(solution)/shard_map/ppermute | solution.py:11
  20.3 4.3 %collective-permute-done.1 = f32[64,1536]{1,0:T(8,128)S(1)} collective-permute-done((f32[64,1536]{1,0:T(8,128)}, f32[64,1536]{1,0:T(8,128)S(1)}, u32[]{:S(2)}, u32[]{:S(2)}) %collective-permute-start.1) | collective-permute-done | bytes 393248 | tf_op jit(solution)/shard_map/ppermute | solution.py:11
  24.6 36.4 %while.10 = (s32[]{:T(128)}, f32[8,8,4096]{2,1,0:T(8,128)}, f32[8,8,1536]{2,1,0:T(8,128)}, f32[64,1536]{1,0:T(8,128)S(1)}, f32[64,1536]{1,0:T(8,128)S(1)}, /*index=5*/s32[]{:T(128)}) while((s32[]{:T(128)}, f32[8,8,4096]{2,1,0:T(8,128)}, f32[8,8,1536]{2,1,0:T(8,128)}, f32[64,1536]{1,0:T(8,128)S(1)}, f32[64,1536]{1,0:T(8,128)S(1)}, ...), condition=%wide.region_1.2_spmd, body=%wide.region_0.1_spmd.sunk | while | flops 604766208 | bytes 7881289 | solution.py:32
  24.6 0.8 dynamic-slice_bitcast_fusion.2
  25.4 0.4 broadcast_multiply_fusion.3
  25.8 2.6 %fusion.8 = f32[512,64]{1,0:T(8,128)S(1)} fusion(f32[512,1536]{1,0:T(8,128)S(1)} %bitcast.27, f32[64,1536]{1,0:T(8,128)S(1)} %get-tuple-element.87), kind=kOutput, calls=%fused_computation.5.clone.1 | convolution fusion | flops 603979776 | bytes 3670016 | tf_op jit(solution)/shard_map/while/body/eval_jaxpr/dot_general | solution.py:23
  28.4 0.1 broadcast_in_dim.11
  28.5 0.7 constant_dynamic-update-slice_fusion.2
  29.2 0.8 dynamic-slice_bitcast_fusion.2
  30.0 0.4 broadcast_multiply_fusion.3
  30.4 2.6 %fusion.8 = f32[512,64]{1,0:T(8,128)S(1)} fusion(f32[512,1536]{1,0:T(8,128)S(1)} %bitcast.27, f32[64,1536]{1,0:T(8,128)S(1)} %get-tuple-element.87), kind=kOutput, calls=%fused_computation.5.clone.1 | convolution fusion | flops 603979776 | bytes 3670016 | tf_op jit(solution)/shard_map/while/body/eval_jaxpr/dot_general | solution.py:23
  33.0 0.1 broadcast_in_dim.11
  33.1 0.7 constant_dynamic-update-slice_fusion.2
  33.7 0.8 dynamic-slice_bitcast_fusion.2
  34.5 0.4 broadcast_multiply_fusion.3
  34.9 2.6 %fusion.8 = f32[512,64]{1,0:T(8,128)S(1)} fusion(f32[512,1536]{1,0:T(8,128)S(1)} %bitcast.27, f32[64,1536]{1,0:T(8,128)S(1)} %get-tuple-element.87), kind=kOutput, calls=%fused_computation.5.clone.1 | convolution fusion | flops 603979776 | bytes 3670016 | tf_op jit(solution)/shard_map/while/body/eval_jaxpr/dot_general | solution.py:23
  37.5 0.1 broadcast_in_dim.11
  37.6 0.7 constant_dynamic-update-slice_fusion.2
  38.3 0.8 dynamic-slice_bitcast_fusion.2
  39.1 0.4 broadcast_multiply_fusion.3
  39.5 2.6 %fusion.8 = f32[512,64]{1,0:T(8,128)S(1)} fusion(f32[512,1536]{1,0:T(8,128)S(1)} %bitcast.27, f32[64,1536]{1,0:T(8,128)S(1)} %get-tuple-element.87), kind=kOutput, calls=%fused_computation.5.clone.1 | convolution fusion | flops 603979776 | bytes 3670016 | tf_op jit(solution)/shard_map/while/body/eval_jaxpr/dot_general | solution.py:23
  42.1 0.1 broadcast_in_dim.11
  42.2 0.7 constant_dynamic-update-slice_fusion.2
  42.8 0.8 dynamic-slice_bitcast_fusion.2
  43.6 0.4 broadcast_multiply_fusion.3
  44.0 2.6 %fusion.8 = f32[512,64]{1,0:T(8,128)S(1)} fusion(f32[512,1536]{1,0:T(8,128)S(1)} %bitcast.27, f32[64,1536]{1,0:T(8,128)S(1)} %get-tuple-element.87), kind=kOutput, calls=%fused_computation.5.clone.1 | convolution fusion | flops 603979776 | bytes 3670016 | tf_op jit(solution)/shard_map/while/body/eval_jaxpr/dot_general | solution.py:23
  46.6 0.1 broadcast_in_dim.11
  46.7 0.7 constant_dynamic-update-slice_fusion.2
  47.4 0.8 dynamic-slice_bitcast_fusion.2
  48.2 0.4 broadcast_multiply_fusion.3
  48.6 2.6 %fusion.8 = f32[512,64]{1,0:T(8,128)S(1)} fusion(f32[512,1536]{1,0:T(8,128)S(1)} %bitcast.27, f32[64,1536]{1,0:T(8,128)S(1)} %get-tuple-element.87), kind=kOutput, calls=%fused_computation.5.clone.1 | convolution fusion | flops 603979776 | bytes 3670016 | tf_op jit(solution)/shard_map/while/body/eval_jaxpr/dot_general | solution.py:23
  51.2 0.1 broadcast_in_dim.11
  51.3 0.7 constant_dynamic-update-slice_fusion.2
  51.9 0.8 dynamic-slice_bitcast_fusion.2
  52.7 0.4 broadcast_multiply_fusion.3
  53.1 2.6 %fusion.8 = f32[512,64]{1,0:T(8,128)S(1)} fusion(f32[512,1536]{1,0:T(8,128)S(1)} %bitcast.27, f32[64,1536]{1,0:T(8,128)S(1)} %get-tuple-element.87), kind=kOutput, calls=%fused_computation.5.clone.1 | convolution fusion | flops 603979776 | bytes 3670016 | tf_op jit(solution)/shard_map/while/body/eval_jaxpr/dot_general | solution.py:23
  55.7 0.1 broadcast_in_dim.11
  55.8 0.7 constant_dynamic-update-slice_fusion.2
  56.5 0.8 dynamic-slice_bitcast_fusion.2
  57.3 0.4 broadcast_multiply_fusion.3
  57.7 2.6 %fusion.8 = f32[512,64]{1,0:T(8,128)S(1)} fusion(f32[512,1536]{1,0:T(8,128)S(1)} %bitcast.27, f32[64,1536]{1,0:T(8,128)S(1)} %get-tuple-element.87), kind=kOutput, calls=%fused_computation.5.clone.1 | convolution fusion | flops 603979776 | bytes 3670016 | tf_op jit(solution)/shard_map/while/body/eval_jaxpr/dot_general | solution.py:23
  60.3 0.1 broadcast_in_dim.11
  60.4 0.7 constant_dynamic-update-slice_fusion.2
  61.0 0.0 reduce-scatter.2.cloned.1.call-update
  61.1 29.4 %reduce-scatter.2.cloned.1.call-done = f32[16,4096]{1,0:T(8,128)} async-done(((f32[64,4096]{1,0:T(8,128)}), f32[16,4096]{1,0:T(8,128)}) %reduce-scatter.2.cloned.1.call-update) | async-done | bytes 262160 | tf_op jit(solution)/shard_map/reduce_scatter | solution.py:43
  90.4 1.0 broadcast_multiply_fusion.1
  91.4 0.0 copy-start
  91.4 0.1 collective-permute-start.2
  91.5 6.7 %collective-permute-done.2 = f32[16,4096]{1,0:T(8,128)S(1)} collective-permute-done((f32[16,4096]{1,0:T(8,128)S(1)}, f32[16,4096]{1,0:T(8,128)S(1)}, u32[]{:S(2)}, u32[]{:S(2)}) %collective-permute-start.2) | collective-permute-done | bytes 262176 | tf_op jit(solution)/shard_map/ppermute | solution.py:11
  98.2 10.1 %all_to_all.15 = f32[16,4,1024]{2,0,1:T(8,128)S(1)} all-to-all(f32[16,4,1024]{2,0,1:T(8,128)S(1)} %bitcast.31), channel_id=1, replica_groups=mesh['vec'=8,'field'=4] {'field'}, dimensions={1} | all-to-all | bytes 524288 | tf_op jit(solution)/shard_map/all_to_all | solution.py:50
  108.3 0.1 reshape.32
  108.5 0.2 copy.7
  108.6 0.9 reshape.33
  109.5 0.0 copy-done
  (2 shorter events, 0.0 us)
Async XLA Ops:
  7.2 83.3 %reduce-scatter.2.cloned.1.call-start = ((), (), s32[]{:S(2)}) async-start(), calls=%async_computation.2 | async-start | bytes 1310720 | tf_op jit(solution)/shard_map/reduce_scatter | solution.py:43
  7.2 13.1 %collective-permute-start = (f32[64,1536]{1,0:T(8,128)}, f32[64,1536]{1,0:T(8,128)S(1)}, u32[]{:S(2)}, u32[]{:S(2)}) collective-permute-start(f32[64,1536]{1,0:T(8,128)} %param.3), channel_id=1, source_target_pairs={{0,28},{4,0},{8,4},{12,8},{16,12},{20,16},{24,20},{28,24},{1,29},{... | collective-permute-start | bytes 1179656 | tf_op jit(solution)/shard_map/ppermute | solution.py:11
  10.6 14.0 %collective-permute-start.1 = (f32[64,1536]{1,0:T(8,128)}, f32[64,1536]{1,0:T(8,128)S(1)}, u32[]{:S(2)}, u32[]{:S(2)}) collective-permute-start(f32[64,1536]{1,0:T(8,128)} %param.3), channel_id=1, source_target_pairs={{0,24},{4,28},{8,0},{12,4},{16,8},{20,12},{24,16},{28,20},{1,25},{... | collective-permute-start | bytes 1179656 | tf_op jit(solution)/shard_map/ppermute | solution.py:11
  91.4 18.1 %copy-start = (f32[16,4096]{1,0:T(8,128)}, f32[16,4096]{1,0:T(8,128)S(1)}, u32[]{:S(2)}) copy-start(f32[16,4096]{1,0:T(8,128)S(1)} %broadcast_multiply_fusion.1) | copy-start | bytes 786436
  91.4 6.7 %collective-permute-start.2 = (f32[16,4096]{1,0:T(8,128)S(1)}, f32[16,4096]{1,0:T(8,128)S(1)}, u32[]{:S(2)}, u32[]{:S(2)}) collective-permute-start(f32[16,4096]{1,0:T(8,128)S(1)} %broadcast_multiply_fusion.1), channel_id=1, source_target_pairs={{0,4},{4,8},{8,12},{12,16},{16,20},{20,24},{24,28},{28,0},{1,5},{5... | collective-permute-start | bytes 786440 | tf_op jit(solution)/shard_map/ppermute | solution.py:11
Sparse Core Ops, SparseCore 0:
  61.2 29.2 reduce-scatter.1
where the time goes:
time: 117 us; the launch traced here: 116 us
  waiting for transfers between devices  49.5 us (42%)
  matrix products  20.7 us (18%)
  between operations  14.1 us (12%)
  local copies, waits for them, and re-layouts  13.8 us (12%)
  blocking collectives  10.1 us (9%)
  starting transfers between devices  4.11 us (4%)
  other arithmetic  3.93 us (3%)
    reduce_scatter x1, waiting for transfers between devices, per_device(): lax.psum_scatter(triple_rows(vectors, following, further), 'field', scatt...  29.4 us
    dot_general x8, matrix products, single_group(): lax.dot_general(product, third, (((1,), (1,)), ((), ())), precision=lax.P...  20.7 us
    ppermute x3, waiting for transfers between devices, passed_along(): return lax.ppermute(x, axis, [(i, (i + by) % peers) for i in range(peers)])  20.1 us
    all_to_all x1, blocking collectives, per_device(): lax.all_to_all(earlier, 'field', split_axis=1, concat_axis=0, tiled=True)  10.1 us
    mul x8, local copies, waits for them, and re-layouts, single_group(): group[:, None, :] * partner[None, :, :]  6.41 us
    dynamic_update_slice x8, local copies, waits for them, and re-layouts, triple_rows(): lax.map(single_group, groups)  5.28 us
    ppermute x3, starting transfers between devices, passed_along(): return lax.ppermute(x, axis, [(i, (i + by) % peers) for i in range(peers)])  4.07 us
    mul x8, other arithmetic, single_group(): group[:, None, :] * partner[None, :, :]  2.95 us
  transfers between devices with their start and end apart: 4, of which 4 were waited for; matrix products, arithmetic and copies ran while one was open for 0% of the time, Pallas kernels for 0%

commit v1 on v0

v1 whole, which is shorter than its diff:
```python
import functools
import math

import jax
import jax.numpy as jnp
from jax import lax
from jax.experimental import pallas as pl
from jax.experimental.pallas import tpu as pltpu
from jax.sharding import PartitionSpec as P

MESH = pl.DeviceIdType.MESH
GATHER_PARTS = 4
TILE_COLUMNS = 256


def kernel(
    peers,
    parts,
    chunks,
    scale,
    own_ref,
    first_ref,
    second_ref,
    next_ref,
    third_ref,
    split_ref,
    partial,
    up,
    down,
    finished,
    next_send,
    next_recv,
    third_send,
    third_recv,
    up_send,
    up_recv,
    down_send,
    down_recv,
    out_send,
    out_recv,
):
    v = lax.axis_index("vec")
    z = lax.axis_index("field")
    after = lax.rem(v + 1, peers)
    before = lax.rem(v + peers - 1, peers)
    rows = own_ref.shape[0]
    owned = rows // parts
    width = first_ref.shape[1] // chunks
    per_chunk = rows // chunks
    per_group = chunks // parts
    last = parts - 1
    piece = rows // GATHER_PARTS

    barrier = pltpu.get_barrier_semaphore()
    for other in range(parts):
        for side in (before, after):
            pl.semaphore_signal(barrier, inc=1, device_id=(side, other), device_id_type=MESH)

    for near in (lax.rem(z + 1, parts), lax.rem(z + last, parts)):
        pl.semaphore_signal(barrier, inc=1, device_id=(v, near), device_id_type=MESH)
    pl.semaphore_wait(barrier, 2 * parts + 2)

    def next_copy(q):
        part = pl.ds(q * piece, piece)
        return pltpu.make_async_remote_copy(
            own_ref.at[part], next_ref.at[part], next_send.at[q], next_recv.at[q],
            device_id=(before, z), device_id_type=MESH,
        )

    def third_copy(q):
        part = pl.ds(q * piece, piece)
        return pltpu.make_async_remote_copy(
            next_ref.at[part], third_ref.at[part], third_send.at[q], third_recv.at[q],
            device_id=(before, z), device_id_type=MESH,
        )

    for q in range(GATHER_PARTS):
        next_copy(q).start()
    own = own_ref[...]
    high = own.astype(jnp.bfloat16)
    split_ref[0:rows] = high
    split_ref[rows : 2 * rows] = (own - high.astype(jnp.float32)).astype(jnp.bfloat16)
    for q in range(GATHER_PARTS):
        next_copy(q).wait_recv()
        third_copy(q).start()
    for q in range(GATHER_PARTS):
        third_copy(q).wait_recv()

    def up_copy(c, g, source):
        return pltpu.make_async_remote_copy(
            source.at[c, g], up.at[c, g], up_send.at[c, g], up_recv.at[c, g],
            device_id=(v, lax.rem(z + 1, parts)), device_id_type=MESH,
        )

    def down_copy(c, g, source):
        return pltpu.make_async_remote_copy(
            source.at[c, g], down.at[c, g], down_send.at[c, g], down_recv.at[c, g],
            device_id=(v, lax.rem(z + last, parts)), device_id_type=MESH,
        )

    def out_copy(c):
        return pltpu.make_async_remote_copy(
            finished.at[c], second_ref.at[z, lax.rem(c, per_group)], out_send.at[c],
            out_recv.at[z, lax.rem(c, per_group)],
            device_id=(after, c // per_group), device_id_type=MESH,
        )

    joined = min(TILE_COLUMNS // rows, per_chunk) if rows < TILE_COLUMNS else 1
    contract = (((1,), (1,)), ((), ()))

    def compute(c, carry):
        for t in range(per_chunk // joined):
            third = third_ref[...]
            base = c * per_chunk + t * joined
            product = jnp.concatenate(
                [next_ref[pl.ds(base + n, 1), :] * third for n in range(joined)], axis=0
            )
            top = product.astype(jnp.bfloat16)
            rest = (product - top.astype(jnp.float32)).astype(jnp.bfloat16)
            both = lax.dot_general(split_ref[...], top, contract, preferred_element_type=jnp.float32)
            small = lax.dot_general(
                split_ref[0:rows], rest, contract, preferred_element_type=jnp.float32
            )
            total = both[0:rows] + (both[rows : 2 * rows] + small)
            span = joined * rows
            for g in range(parts):
                partial[c, g, :, t * span : (t + 1) * span] = total[g * owned : (g + 1) * owned]

        @pl.when(z == 0)
        def _():
            for g in range(1, parts):
                up_copy(c, g, partial).start()

        @pl.when(z == last)
        def _():
            for g in range(last):
                down_copy(c, g, partial).start()

        return carry

    lax.fori_loop(0, chunks, compute, 0)

    def step(s, carry):
        rising = s - z + 1

        @pl.when(jnp.logical_and(z > 0, jnp.logical_and(rising >= 0, rising < chunks)))
        def _():
            def forward(g, carry):
                up_copy(rising, g, up).wait_recv()
                up[rising, g] = up[rising, g] + partial[rising, g]
                up_copy(rising, g, up).start()
                return carry

            lax.fori_loop(z + 1, parts, forward, 0)

        falling = s - (last - z) + 1

        @pl.when(jnp.logical_and(z < last, jnp.logical_and(falling >= 0, falling < chunks)))
        def _():
            def forward(g, carry):
                down_copy(falling, g, down).wait_recv()
                down[falling, g] = down[falling, g] + partial[falling, g]
                down_copy(falling, g, down).start()
                return carry

            lax.fori_loop(0, z, forward, 0)

        done = s - last + 1

        @pl.when(jnp.logical_and(done >= 0, done < chunks))
        def _():
            @pl.when(z > 0)
            def _():
                up_copy(done, z, up).wait_recv()
                partial[done, z] = partial[done, z] + up[done, z]

            @pl.when(z < last)
            def _():
                down_copy(done, z, down).wait_recv()
                partial[done, z] = partial[done, z] + down[done, z]

            result = partial[done, z] * scale
            finished[done] = result
            out_copy(done).start()
            first_ref[:, pl.ds(pl.multiple_of(done * width, width), width)] = result

        return carry

    lax.fori_loop(0, chunks + last, step, 0)

    for q in range(GATHER_PARTS):
        next_copy(q).wait_send()
        third_copy(q).wait_send()

    def drain(c, carry):
        def rise(g, carry):
            up_copy(c, g, up).wait_send()
            return carry

        def fall(g, carry):
            down_copy(c, g, down).wait_send()
            return carry

        lax.fori_loop(z + 1, parts, rise, 0)
        lax.fori_loop(0, z, fall, 0)
        out_copy(c).wait_send()
        return carry

    lax.fori_loop(0, chunks, drain, 0)

    for source in range(parts):
        for sub in range(per_group):
            pltpu.make_async_remote_copy(
                finished.at[0], second_ref.at[source, sub], out_send.at[0],
                out_recv.at[source, sub], device_id=(after, z), device_id_type=MESH,
            ).wait_recv()


def per_device(vectors):
    peers = lax.axis_size("vec")
    parts = lax.axis_size("field")
    rows, fields = vectors.shape
    owned = rows // parts
    chunks = max(8, parts)
    width = rows * rows // chunks
    scale = 1.0 / math.sqrt(fields * parts)
    per_group = chunks // parts
    vmem = pl.BlockSpec(memory_space=pltpu.VMEM)
    dma = pltpu.SemaphoreType.DMA
    first, second = pl.pallas_call(
        functools.partial(kernel, peers, parts, chunks, scale),
        out_shape=(
            jax.ShapeDtypeStruct((owned, rows * rows), jnp.float32),
            jax.ShapeDtypeStruct((parts, per_group, owned, width), jnp.float32),
        ),
        in_specs=[vmem],
        out_specs=(vmem, vmem),
        scratch_shapes=[
            pltpu.VMEM((rows, fields), jnp.float32),
            pltpu.VMEM((rows, fields), jnp.float32),
            pltpu.VMEM((2 * rows, fields), jnp.bfloat16),
            pltpu.VMEM((chunks, parts, owned, width), jnp.float32),
            pltpu.VMEM((chunks, parts, owned, width), jnp.float32),
            pltpu.VMEM((chunks, parts, owned, width), jnp.float32),
            pltpu.VMEM((chunks, owned, width), jnp.float32),
            dma((GATHER_PARTS,)),
            dma((GATHER_PARTS,)),
            dma((GATHER_PARTS,)),
            dma((GATHER_PARTS,)),
            dma((chunks, parts)),
            dma((chunks, parts)),
            dma((chunks, parts)),
            dma((chunks, parts)),
            dma((chunks,)),
            dma((parts, per_group)),
        ],
        compiler_params=pltpu.CompilerParams(
            collective_id=0, has_side_effects=True, vmem_limit_bytes=48 * 1024 * 1024
        ),
    )(vectors)
    second = second.reshape(parts, per_group, owned, width // rows, rows)
    second = second.transpose(1, 3, 0, 2, 4).reshape(owned, rows * rows)
    return (first, second)


def solution(mesh):
    return jax.shard_map(
        per_device,
        mesh=mesh,
        in_specs=(P("vec", "field"),),
        out_specs=(P(("vec", "field"), None), P(("vec", "field"), None)),
        check_vma=False,
    )
```

time: 117 us -> 55.4 us (0.47)
  the two profiles are of different devices: /device:TPU:0 before, /device:TPU:24 now
where the time goes in v1:
time: 55.4 us; the launch traced here: 55.3 us
  Pallas kernels  51.8 us (94%)
  local copies, waits for them, and re-layouts  2.82 us (5%)
  between operations  0.65 us (1%)
    pallas_call x1, Pallas kernels, per_device(): pl.pallas_call(functools.partial(kernel, peers, parts, chunks, scale), ou...  51.8 us
    unnamed x3, local copies, waits for them, and re-layouts  1.69 us

profile of v1, /device:TPU:24, one launch (start us, length us, event | category | flops | bytes accessed | tf_op | source)
XLA Modules:
  0.0 55.3 jit_solution(6547373734352749633)
XLA Ops:
  0.6 0.0 copy-start
  0.6 1.0 %copy-done = f32[64,1536]{1,0:T(8,128)S(1)} copy-done((f32[64,1536]{1,0:T(8,128)S(1)}, f32[64,1536]{1,0:T(8,128)}, u32[]{:S(2)}) %copy-start) | copy-done | bytes 393240
  1.6 51.8 %shard_map.30 = (f32[16,4096]{1,0:T(8,128)S(1)}, f32[4,2,16,512]{3,2,1,0:T(8,128)S(1)}) custom-call(f32[64,1536]{1,0:T(8,128)S(1)} %copy-done), custom_call_target="tpu_custom_call" | custom-call | tf_op jit(solution)/shard_map/pallas_call | solution.py:230
  53.4 0.1 reshape.10
  53.6 0.1 copy.3
  53.7 0.9 %reshape.11 = f32[16,4096]{1,0:T(8,128)} reshape(f32[2,8,4,16,64]{4,3,2,1,0:T(8,128)S(1)} %copy.3) | data formatting | bytes 524288 | tf_op jit(solution)/shard_map/reshape | solution.py:262
  54.6 0.7 %copy.5 = f32[16,4096]{1,0:T(8,128)} copy(f32[16,4096]{1,0:T(8,128)S(1)} %get-tuple-element.8) | data formatting | bytes 524288
Async XLA Ops:
  0.6 1.0 %copy-start = (f32[64,1536]{1,0:T(8,128)S(1)}, f32[64,1536]{1,0:T(8,128)}, u32[]{:S(2)}) copy-start(f32[64,1536]{1,0:T(8,128)} %own_ref.1) | copy-start | bytes 1179652

commit v2 on v1

--- a/solution.py
+++ b/solution.py
@@ -11,6 +11,7 @@
 MESH = pl.DeviceIdType.MESH
 GATHER_PARTS = 4
 TILE_COLUMNS = 256
+LAG = 2
 
 
 def kernel(
@@ -128,7 +129,7 @@
 
         @pl.when(z == 0)
         def _():
-            for g in range(1, parts):
+            for g in range(last, 0, -1):
                 up_copy(c, g, partial).start()
 
         @pl.when(z == last)
@@ -138,20 +139,19 @@
 
         return carry
 
-    lax.fori_loop(0, chunks, compute, 0)
-
     def step(s, carry):
         rising = s - z + 1
 
         @pl.when(jnp.logical_and(z > 0, jnp.logical_and(rising >= 0, rising < chunks)))
         def _():
-            def forward(g, carry):
+            def forward(n, carry):
+                g = last - n
                 up_copy(rising, g, up).wait_recv()
                 up[rising, g] = up[rising, g] + partial[rising, g]
                 up_copy(rising, g, up).start()
                 return carry
 
-            lax.fori_loop(z + 1, parts, forward, 0)
+            lax.fori_loop(0, last - z, forward, 0)
 
         falling = s - (last - z) + 1
 
@@ -186,7 +186,14 @@
 
         return carry
 
-    lax.fori_loop(0, chunks + last, step, 0)
+    def both_at(s, carry):
+        @pl.when(s < chunks)
+        def _():
+            compute(s, 0)
+
+        return step(s - LAG, carry)
+
+    lax.fori_loop(0, chunks + last + LAG, both_at, 0)
 
     for q in range(GATHER_PARTS):
         next_copy(q).wait_send()

time: 55.4 us -> 47.8 us (0.86)
  Pallas kernels: 51.8 us -> 44.2 us
    pallas_call x1, Pallas kernels: 51.8 us -> 44.2 us  [per_device(): pl.pallas_call(functools.partial(kernel, peers, parts, chunks, scale), ou...]
where the time goes in v2:
time: 47.8 us; the launch traced here: 47.7 us
  Pallas kernels  44.2 us (92%)
  local copies, waits for them, and re-layouts  2.82 us (6%)
  between operations  0.65 us (1%)
    pallas_call x1, Pallas kernels, per_device(): pl.pallas_call(functools.partial(kernel, peers, parts, chunks, scale), ou...  44.2 us
    unnamed x3, local copies, waits for them, and re-layouts  1.69 us

profile of v2, /device:TPU:24, one launch (start us, length us, event | category | flops | bytes accessed | tf_op | source)
XLA Modules:
  0.0 47.7 jit_solution(15195739578496899577)
XLA Ops:
  0.6 0.0 copy-start
  0.6 1.0 %copy-done = f32[64,1536]{1,0:T(8,128)S(1)} copy-done((f32[64,1536]{1,0:T(8,128)S(1)}, f32[64,1536]{1,0:T(8,128)}, u32[]{:S(2)}) %copy-start) | copy-done | bytes 393240
  1.6 44.2 %shard_map.30 = (f32[16,4096]{1,0:T(8,128)S(1)}, f32[4,2,16,512]{3,2,1,0:T(8,128)S(1)}) custom-call(f32[64,1536]{1,0:T(8,128)S(1)} %copy-done), custom_call_target="tpu_custom_call" | custom-call | tf_op jit(solution)/shard_map/pallas_call | solution.py:237
  45.8 0.1 reshape.10
  46.0 0.1 copy.3
  46.1 0.9 %reshape.11 = f32[16,4096]{1,0:T(8,128)} reshape(f32[2,8,4,16,64]{4,3,2,1,0:T(8,128)S(1)} %copy.3) | data formatting | bytes 524288 | tf_op jit(solution)/shard_map/reshape | solution.py:269
  47.0 0.7 %copy.5 = f32[16,4096]{1,0:T(8,128)} copy(f32[16,4096]{1,0:T(8,128)S(1)} %get-tuple-element.8) | data formatting | bytes 524288
Async XLA Ops:
  0.6 1.0 %copy-start = (f32[64,1536]{1,0:T(8,128)S(1)}, f32[64,1536]{1,0:T(8,128)}, u32[]{:S(2)}) copy-start(f32[64,1536]{1,0:T(8,128)} %own_ref.1) | copy-start | bytes 1179652

commit v3 on v2

--- a/solution.py
+++ b/solution.py
@@ -11,7 +11,7 @@
 MESH = pl.DeviceIdType.MESH
 GATHER_PARTS = 4
 TILE_COLUMNS = 256
-LAG = 2
+LAG = 3
 
 
 def kernel(
@@ -61,6 +61,9 @@
         pl.semaphore_signal(barrier, inc=1, device_id=(v, near), device_id_type=MESH)
     pl.semaphore_wait(barrier, 2 * parts + 2)
 
+    def place(c):
+        return lax.rem(c, parts) * per_group + c // parts
+
     def next_copy(q):
         part = pl.ds(q * piece, piece)
         return pltpu.make_async_remote_copy(
@@ -101,9 +104,9 @@
 
     def out_copy(c):
         return pltpu.make_async_remote_copy(
-            finished.at[c], second_ref.at[z, lax.rem(c, per_group)], out_send.at[c],
-            out_recv.at[z, lax.rem(c, per_group)],
-            device_id=(after, c // per_group), device_id_type=MESH,
+            finished.at[c], second_ref.at[z, c // parts], out_send.at[c],
+            out_recv.at[z, c // parts],
+            device_id=(after, lax.rem(c, parts)), device_id_type=MESH,
         )
 
     joined = min(TILE_COLUMNS // rows, per_chunk) if rows < TILE_COLUMNS else 1
@@ -112,7 +115,7 @@
     def compute(c, carry):
         for t in range(per_chunk // joined):
             third = third_ref[...]
-            base = c * per_chunk + t * joined
+            base = place(c) * per_chunk + t * joined
             product = jnp.concatenate(
                 [next_ref[pl.ds(base + n, 1), :] * third for n in range(joined)], axis=0
             )
@@ -182,7 +185,7 @@
             result = partial[done, z] * scale
             finished[done] = result
             out_copy(done).start()
-            first_ref[:, pl.ds(pl.multiple_of(done * width, width), width)] = result
+            first_ref[:, pl.ds(pl.multiple_of(place(done) * width, width), width)] = result
 
         return carry
 
@@ -228,7 +231,7 @@
     parts = lax.axis_size("field")
     rows, fields = vectors.shape
     owned = rows // parts
-    chunks = max(8, parts)
+    chunks = max(16, parts)
     width = rows * rows // chunks
     scale = 1.0 / math.sqrt(fields * parts)
     per_group = chunks // parts

time: 47.8 us -> 59 us (1.23)
  the two profiles are of different devices: /device:TPU:24 before, /device:TPU:0 now
where the time goes in v3:
time: 59 us; the launch traced here: 58.9 us
  Pallas kernels  55.3 us (94%)
  local copies, waits for them, and re-layouts  2.87 us (5%)
  between operations  0.66 us (1%)
    pallas_call x1, Pallas kernels, per_device(): pl.pallas_call(functools.partial(kernel, peers, parts, chunks, scale), ou...  55.3 us
    unnamed x3, local copies, waits for them, and re-layouts  1.69 us

profile of v3, /device:TPU:0, one launch (start us, length us, event | category | flops | bytes accessed | tf_op | source)
XLA Modules:
  0.0 58.9 jit_solution(16347334879015989694)
XLA Ops:
  0.6 0.0 copy-start
  0.6 1.0 %copy-done = f32[64,1536]{1,0:T(8,128)S(1)} copy-done((f32[64,1536]{1,0:T(8,128)S(1)}, f32[64,1536]{1,0:T(8,128)}, u32[]{:S(2)}) %copy-start) | copy-done | bytes 393240
  1.6 55.3 %shard_map.30 = (f32[16,4096]{1,0:T(8,128)S(1)}, f32[4,4,16,256]{3,2,1,0:T(8,128)S(1)}) custom-call(f32[64,1536]{1,0:T(8,128)S(1)} %copy-done), custom_call_target="tpu_custom_call" | custom-call | tf_op jit(solution)/shard_map/pallas_call | solution.py:240
  57.0 0.2 reshape.10
  57.2 0.1 copy.3
  57.3 0.9 %reshape.11 = f32[16,4096]{1,0:T(8,128)} reshape(f32[4,4,4,16,64]{4,3,2,1,0:T(8,128)S(1)} %copy.3) | data formatting | bytes 524288 | tf_op jit(solution)/shard_map/reshape | solution.py:272
  58.2 0.7 %copy.5 = f32[16,4096]{1,0:T(8,128)} copy(f32[16,4096]{1,0:T(8,128)S(1)} %get-tuple-element.8) | data formatting | bytes 524288
Async XLA Ops:
  0.6 1.0 %copy-start = (f32[64,1536]{1,0:T(8,128)S(1)}, f32[64,1536]{1,0:T(8,128)}, u32[]{:S(2)}) copy-start(f32[64,1536]{1,0:T(8,128)} %own_ref.1) | copy-start | bytes 1179652

commit v4 on v2

--- a/solution.py
+++ b/solution.py
@@ -87,15 +87,15 @@
     for q in range(GATHER_PARTS):
         third_copy(q).wait_recv()
 
-    def up_copy(c, g, source):
-        return pltpu.make_async_remote_copy(
-            source.at[c, g], up.at[c, g], up_send.at[c, g], up_recv.at[c, g],
+    def up_copy(c, d, source):
+        return pltpu.make_async_remote_copy(
+            source.at[c, d + 1 : parts], up.at[c, d + 1 : parts], up_send.at[c], up_recv.at[c],
             device_id=(v, lax.rem(z + 1, parts)), device_id_type=MESH,
         )
 
-    def down_copy(c, g, source):
-        return pltpu.make_async_remote_copy(
-            source.at[c, g], down.at[c, g], down_send.at[c, g], down_recv.at[c, g],
+    def down_copy(c, d, source):
+        return pltpu.make_async_remote_copy(
+            source.at[c, 0:d], down.at[c, 0:d], down_send.at[c], down_recv.at[c],
             device_id=(v, lax.rem(z + last, parts)), device_id_type=MESH,
         )
 
@@ -129,41 +129,35 @@
 
         @pl.when(z == 0)
         def _():
-            for g in range(last, 0, -1):
-                up_copy(c, g, partial).start()
+            up_copy(c, 0, partial).start()
 
         @pl.when(z == last)
         def _():
-            for g in range(last):
-                down_copy(c, g, partial).start()
+            down_copy(c, last, partial).start()
 
         return carry
 
     def step(s, carry):
         rising = s - z + 1
-
-        @pl.when(jnp.logical_and(z > 0, jnp.logical_and(rising >= 0, rising < chunks)))
-        def _():
-            def forward(n, carry):
-                g = last - n
-                up_copy(rising, g, up).wait_recv()
-                up[rising, g] = up[rising, g] + partial[rising, g]
-                up_copy(rising, g, up).start()
-                return carry
-
-            lax.fori_loop(0, last - z, forward, 0)
-
         falling = s - (last - z) + 1
 
-        @pl.when(jnp.logical_and(z < last, jnp.logical_and(falling >= 0, falling < chunks)))
-        def _():
-            def forward(g, carry):
-                down_copy(falling, g, down).wait_recv()
-                down[falling, g] = down[falling, g] + partial[falling, g]
-                down_copy(falling, g, down).start()
-                return carry
-
-            lax.fori_loop(0, z, forward, 0)
+        for d in range(1, parts):
+            @pl.when(jnp.logical_and(z == d, jnp.logical_and(rising >= 0, rising < chunks)))
+            def _(d=d):
+                up_copy(rising, d - 1, up).wait_recv()
+                if d < last:
+                    up[rising, d + 1 : parts] = (
+                        up[rising, d + 1 : parts] + partial[rising, d + 1 : parts]
+                    )
+                    up_copy(rising, d, up).start()
+
+        for d in range(last):
+            @pl.when(jnp.logical_and(z == d, jnp.logical_and(falling >= 0, falling < chunks)))
+            def _(d=d):
+                down_copy(falling, d + 1, down).wait_recv()
+                if d > 0:
+                    down[falling, 0:d] = down[falling, 0:d] + partial[falling, 0:d]
+                    down_copy(falling, d, down).start()
 
         done = s - last + 1
 
@@ -171,12 +165,10 @@
         def _():
             @pl.when(z > 0)
             def _():
-                up_copy(done, z, up).wait_recv()
                 partial[done, z] = partial[done, z] + up[done, z]
 
             @pl.when(z < last)
             def _():
-                down_copy(done, z, down).wait_recv()
                 partial[done, z] = partial[done, z] + down[done, z]
 
             result = partial[done, z] * scale
@@ -200,16 +192,14 @@
         third_copy(q).wait_send()
 
     def drain(c, carry):
-        def rise(g, carry):
-            up_copy(c, g, up).wait_send()
-            return carry
-
-        def fall(g, carry):
-            down_copy(c, g, down).wait_send()
-            return carry
-
-        lax.fori_loop(z + 1, parts, rise, 0)
-        lax.fori_loop(0, z, fall, 0)
+        for d in range(parts):
+            @pl.when(z == d)
+            def _(d=d):
+                if d < last:
+                    up_copy(c, d, up).wait_send()
+                if d > 0:
+                    down_copy(c, d, down).wait_send()
+
         out_copy(c).wait_send()
         return carry
 
@@ -254,10 +244,10 @@
             dma((GATHER_PARTS,)),
             dma((GATHER_PARTS,)),
             dma((GATHER_PARTS,)),
-            dma((chunks, parts)),
-            dma((chunks, parts)),
-            dma((chunks, parts)),
-            dma((chunks, parts)),
+            dma((chunks,)),
+            dma((chunks,)),
+            dma((chunks,)),
+            dma((chunks,)),
             dma((chunks,)),
             dma((parts, per_group)),
         ],

time: 47.8 us -> 51.1 us (1.069)
  Pallas kernels: 44.2 us -> 47.5 us
    pallas_call x1, Pallas kernels: 44.2 us -> 47.5 us  [per_device(): pl.pallas_call(functools.partial(kernel, peers, parts, chunks, scale), ou...]
where the time goes in v4:
time: 51.1 us; the launch traced here: 51 us
  Pallas kernels  47.5 us (93%)
  local copies, waits for them, and re-layouts  2.82 us (6%)
  between operations  0.65 us (1%)
    pallas_call x1, Pallas kernels, per_device(): pl.pallas_call(functools.partial(kernel, peers, parts, chunks, scale), ou...  47.5 us
    unnamed x3, local copies, waits for them, and re-layouts  1.69 us

profile of v4, /device:TPU:24, one launch (start us, length us, event | category | flops | bytes accessed | tf_op | source)
XLA Modules:
  0.0 51.0 jit_solution(159251422710891964)
XLA Ops:
  0.6 0.0 copy-start
  0.6 1.0 %copy-done = f32[64,1536]{1,0:T(8,128)S(1)} copy-done((f32[64,1536]{1,0:T(8,128)S(1)}, f32[64,1536]{1,0:T(8,128)}, u32[]{:S(2)}) %copy-start) | copy-done | bytes 393240
  1.6 47.5 %shard_map.30 = (f32[16,4096]{1,0:T(8,128)S(1)}, f32[4,2,16,512]{3,2,1,0:T(8,128)S(1)}) custom-call(f32[64,1536]{1,0:T(8,128)S(1)} %copy-done), custom_call_target="tpu_custom_call" | custom-call | tf_op jit(solution)/shard_map/pallas_call | solution.py:227
  49.1 0.1 reshape.10
  49.3 0.1 copy.3
  49.4 0.9 %reshape.11 = f32[16,4096]{1,0:T(8,128)} reshape(f32[2,8,4,16,64]{4,3,2,1,0:T(8,128)S(1)} %copy.3) | data formatting | bytes 524288 | tf_op jit(solution)/shard_map/reshape | solution.py:259
  50.2 0.7 %copy.5 = f32[16,4096]{1,0:T(8,128)} copy(f32[16,4096]{1,0:T(8,128)S(1)} %get-tuple-element.8) | data formatting | bytes 524288
Async XLA Ops:
  0.6 1.0 %copy-start = (f32[64,1536]{1,0:T(8,128)S(1)}, f32[64,1536]{1,0:T(8,128)}, u32[]{:S(2)}) copy-start(f32[64,1536]{1,0:T(8,128)} %own_ref.1) | copy-start | bytes 1179652

commit v5 on v2

--- a/solution.py
+++ b/solution.py
@@ -9,9 +9,9 @@
 from jax.sharding import PartitionSpec as P
 
 MESH = pl.DeviceIdType.MESH
-GATHER_PARTS = 4
+GATHER_PARTS = 8
 TILE_COLUMNS = 256
-LAG = 2
+LAG = 3
 
 
 def kernel(

time: 47.8 us -> 48.3 us (1.010)
  Pallas kernels: 44.2 us -> 44.7 us
    pallas_call x1, Pallas kernels: 44.2 us -> 44.7 us  [per_device(): pl.pallas_call(functools.partial(kernel, peers, parts, chunks, scale), ou...]
where the time goes in v5:
time: 48.3 us; the launch traced here: 48.2 us
  Pallas kernels  44.7 us (93%)
  local copies, waits for them, and re-layouts  2.82 us (6%)
  between operations  0.65 us (1%)
    pallas_call x1, Pallas kernels, per_device(): pl.pallas_call(functools.partial(kernel, peers, parts, chunks, scale), ou...  44.7 us
    unnamed x3, local copies, waits for them, and re-layouts  1.69 us

profile of v5, /device:TPU:24, one launch (start us, length us, event | category | flops | bytes accessed | tf_op | source)
XLA Modules:
  0.0 48.2 jit_solution(11851389779407265362)
XLA Ops:
  0.6 0.0 copy-start
  0.6 1.0 %copy-done = f32[64,1536]{1,0:T(8,128)S(1)} copy-done((f32[64,1536]{1,0:T(8,128)S(1)}, f32[64,1536]{1,0:T(8,128)}, u32[]{:S(2)}) %copy-start) | copy-done | bytes 393240
  1.6 44.7 %shard_map.30 = (f32[16,4096]{1,0:T(8,128)S(1)}, f32[4,2,16,512]{3,2,1,0:T(8,128)S(1)}) custom-call(f32[64,1536]{1,0:T(8,128)S(1)} %copy-done), custom_call_target="tpu_custom_call" | custom-call | tf_op jit(solution)/shard_map/pallas_call | solution.py:237
  46.3 0.1 reshape.10
  46.5 0.1 copy.3
  46.6 0.9 %reshape.11 = f32[16,4096]{1,0:T(8,128)} reshape(f32[2,8,4,16,64]{4,3,2,1,0:T(8,128)S(1)} %copy.3) | data formatting | bytes 524288 | tf_op jit(solution)/shard_map/reshape | solution.py:269
  47.5 0.7 %copy.5 = f32[16,4096]{1,0:T(8,128)} copy(f32[16,4096]{1,0:T(8,128)S(1)} %get-tuple-element.8) | data formatting | bytes 524288
Async XLA Ops:
  0.6 1.0 %copy-start = (f32[64,1536]{1,0:T(8,128)S(1)}, f32[64,1536]{1,0:T(8,128)}, u32[]{:S(2)}) copy-start(f32[64,1536]{1,0:T(8,128)} %own_ref.1) | copy-start | bytes 1179652

commit v6 on v2

--- a/solution.py
+++ b/solution.py
@@ -24,6 +24,7 @@
     second_ref,
     next_ref,
     third_ref,
+    local_ref,
     split_ref,
     partial,
     up,
@@ -39,6 +40,7 @@
     down_recv,
     out_send,
     out_recv,
+    local_done,
 ):
     v = lax.axis_index("vec")
     z = lax.axis_index("field")
@@ -52,6 +54,8 @@
     last = parts - 1
     piece = rows // GATHER_PARTS
 
+    local = pltpu.make_async_copy(own_ref, local_ref, local_done)
+    local.start()
     barrier = pltpu.get_barrier_semaphore()
     for other in range(parts):
         for side in (before, after):
@@ -77,7 +81,8 @@
 
     for q in range(GATHER_PARTS):
         next_copy(q).start()
-    own = own_ref[...]
+    local.wait()
+    own = local_ref[...]
     high = own.astype(jnp.bfloat16)
     split_ref[0:rows] = high
     split_ref[rows : 2 * rows] = (own - high.astype(jnp.float32)).astype(jnp.bfloat16)
@@ -240,9 +245,10 @@
             jax.ShapeDtypeStruct((owned, rows * rows), jnp.float32),
             jax.ShapeDtypeStruct((parts, per_group, owned, width), jnp.float32),
         ),
-        in_specs=[vmem],
+        in_specs=[pl.BlockSpec(memory_space=pl.ANY)],
         out_specs=(vmem, vmem),
         scratch_shapes=[
+            pltpu.VMEM((rows, fields), jnp.float32),
             pltpu.VMEM((rows, fields), jnp.float32),
             pltpu.VMEM((rows, fields), jnp.float32),
             pltpu.VMEM((2 * rows, fields), jnp.bfloat16),
@@ -260,6 +266,7 @@
             dma((chunks, parts)),
             dma((chunks,)),
             dma((parts, per_group)),
+            dma,
         ],
         compiler_params=pltpu.CompilerParams(
             collective_id=0, has_side_effects=True, vmem_limit_bytes=48 * 1024 * 1024

time: 47.8 us -> 48 us (level)
  no operation moved by 1% of the time
where the time goes in v6:
time: 48 us; the launch traced here: 47.9 us
  Pallas kernels  44.4 us (92%)
  local copies, waits for them, and re-layouts  2.82 us (6%)
  between operations  0.65 us (1%)
    pallas_call x1, Pallas kernels, per_device(): pl.pallas_call(functools.partial(kernel, peers, parts, chunks, scale), ou...  44.4 us
    unnamed x3, local copies, waits for them, and re-layouts  1.69 us

profile of v6, /device:TPU:24, one launch (start us, length us, event | category | flops | bytes accessed | tf_op | source)
XLA Modules:
  0.0 47.9 jit_solution(17433105450229687569)
XLA Ops:
  0.6 0.0 copy-start
  0.6 1.0 %copy-done = f32[64,1536]{1,0:T(8,128)S(1)} copy-done((f32[64,1536]{1,0:T(8,128)S(1)}, f32[64,1536]{1,0:T(8,128)}, u32[]{:S(2)}) %copy-start) | copy-done | bytes 393240
  1.6 44.4 %shard_map.30 = (f32[16,4096]{1,0:T(8,128)S(1)}, f32[4,2,16,512]{3,2,1,0:T(8,128)S(1)}) custom-call(f32[64,1536]{1,0:T(8,128)S(1)} %copy-done), custom_call_target="tpu_custom_call" | custom-call | tf_op jit(solution)/shard_map/pallas_call | solution.py:242
  46.0 0.1 reshape.10
  46.2 0.1 copy.3
  46.3 0.9 %reshape.11 = f32[16,4096]{1,0:T(8,128)} reshape(f32[2,8,4,16,64]{4,3,2,1,0:T(8,128)S(1)} %copy.3) | data formatting | bytes 524288 | tf_op jit(solution)/shard_map/reshape | solution.py:276
  47.2 0.7 %copy.5 = f32[16,4096]{1,0:T(8,128)} copy(f32[16,4096]{1,0:T(8,128)S(1)} %get-tuple-element.8) | data formatting | bytes 524288
Async XLA Ops:
  0.6 1.0 %copy-start = (f32[64,1536]{1,0:T(8,128)S(1)}, f32[64,1536]{1,0:T(8,128)}, u32[]{:S(2)}) copy-start(f32[64,1536]{1,0:T(8,128)} %own_ref.1) | copy-start | bytes 1179652

commit v7 on v6

--- a/solution.py
+++ b/solution.py
@@ -9,7 +9,7 @@
 from jax.sharding import PartitionSpec as P
 
 MESH = pl.DeviceIdType.MESH
-GATHER_PARTS = 4
+GATHER_PARTS = 2
 TILE_COLUMNS = 256
 LAG = 2
 

time: 48 us -> 49.3 us (1.027)
  Pallas kernels: 44.4 us -> 45.7 us
    pallas_call x1, Pallas kernels: 44.4 us -> 45.7 us  [per_device(): pl.pallas_call(functools.partial(kernel, peers, parts, chunks, scale), ou...]
where the time goes in v7:
time: 49.3 us; the launch traced here: 49.1 us
  Pallas kernels  45.7 us (93%)
  local copies, waits for them, and re-layouts  2.82 us (6%)
  between operations  0.65 us (1%)
    pallas_call x1, Pallas kernels, per_device(): pl.pallas_call(functools.partial(kernel, peers, parts, chunks, scale), ou...  45.7 us
    unnamed x3, local copies, waits for them, and re-layouts  1.69 us

profile of v7, /device:TPU:24, one launch (start us, length us, event | category | flops | bytes accessed | tf_op | source)
XLA Modules:
  0.0 49.1 jit_solution(13028969052127620841)
XLA Ops:
  0.6 0.0 copy-start
  0.6 1.0 %copy-done = f32[64,1536]{1,0:T(8,128)S(1)} copy-done((f32[64,1536]{1,0:T(8,128)S(1)}, f32[64,1536]{1,0:T(8,128)}, u32[]{:S(2)}) %copy-start) | copy-done | bytes 393240
  1.6 45.7 %shard_map.30 = (f32[16,4096]{1,0:T(8,128)S(1)}, f32[4,2,16,512]{3,2,1,0:T(8,128)S(1)}) custom-call(f32[64,1536]{1,0:T(8,128)S(1)} %copy-done), custom_call_target="tpu_custom_call" | custom-call | tf_op jit(solution)/shard_map/pallas_call | solution.py:242
  47.3 0.1 reshape.10
  47.4 0.1 copy.3
  47.5 0.9 %reshape.11 = f32[16,4096]{1,0:T(8,128)} reshape(f32[2,8,4,16,64]{4,3,2,1,0:T(8,128)S(1)} %copy.3) | data formatting | bytes 524288 | tf_op jit(solution)/shard_map/reshape | solution.py:276
  48.4 0.7 %copy.5 = f32[16,4096]{1,0:T(8,128)} copy(f32[16,4096]{1,0:T(8,128)S(1)} %get-tuple-element.8) | data formatting | bytes 524288
Async XLA Ops:
  0.6 1.0 %copy-start = (f32[64,1536]{1,0:T(8,128)S(1)}, f32[64,1536]{1,0:T(8,128)}, u32[]{:S(2)}) copy-start(f32[64,1536]{1,0:T(8,128)} %own_ref.1) | copy-start | bytes 1179652
